TPU v7x, 32 devices: a whole 2x2x4 slice. The times are simulated.
32 devices in a mesh: grp: 2 (over y), beam: 4 (over z), slab: 2 (over x), pol: 2 (over core).
Axes of the slice: x: 2, y: 2, z: 4, core: 2. Of those that a mesh axis runs over, the one named last changes fastest.
Arguments:
- stokes: bfloat16 [2, 1024, 16384], P('pol', 'grp', ('beam', 'slab')), parts along dimension 1, may hold values from -6 to 6
- lambda_sq: float32 [16384], replicated, may hold values from 0.005 to 0.1
- channel_flags: int32 [16384], replicated, may hold values from 0 to 1, as said below
- counts: int32 [1024], P('grp'), parts along dimension 0, may hold values from 1 to 4
Outputs:
- spectrum: float32 [1024, 2048], P(('grp', 'beam', 'slab', 'pol')), parts along dimension 0
There are 2 independent parts, one for each index of `grp`. A program takes and returns all parts, laid end to end along the dimension named above; an argument that names none is the same for every part. Nothing has to cross between parts.
Inputs may be any that keep to these rules, and one draw needn't show every extreme that they name: `channel_flags`: at least one channel is kept.
All inputs are finite; a program needn't handle non-finite values.
Results may differ from a plain program's by a relative error of at most 0.0032.
Values may be sent and summed in bfloat16 or wider, within the bound.
A program may use at most 64 MiB of HBM per device.

v0:
```python
import jax
import jax.numpy as jnp
from jax import lax
from jax.sharding import PartitionSpec as P

NPHI = 1024
DEPTH_BLOCK = 128


depth_step = 32.0


def depth_values(depth_ids):
    return depth_step * (depth_ids.astype(jnp.float32) - NPHI // 2)


def build_table(lambda_block, flag_block, norm_scale, center, depths, first_pol):
    phases = (2.0 * depths)[None, :] * (lambda_block - center)[:, None]
    weight = (norm_scale * flag_block)[:, None]
    cos_part = weight * jnp.cos(phases)
    sin_part = weight * jnp.sin(phases)
    first_table = jnp.where(first_pol, cos_part, sin_part).astype(jnp.bfloat16)
    second_table = jnp.where(first_pol, -sin_part, cos_part).astype(jnp.bfloat16)
    return jnp.concatenate([first_table, second_table], 1)


def synth_dense(turned, lambda_local, flag_local, norm_scale, center, first_pol):
    row_count, chan_count = turned.shape
    block_width = min(1024, chan_count)
    block_count = chan_count // block_width
    depths = depth_values(jnp.arange(NPHI, dtype=jnp.int32))

    def add_block(index, totals):
        offset = index * block_width
        block = lax.dynamic_slice_in_dim(turned, offset, block_width, 1)
        lambda_block = lax.dynamic_slice_in_dim(lambda_local, offset, block_width, 0)
        flag_block = lax.dynamic_slice_in_dim(flag_local, offset, block_width, 0)
        phase_table = build_table(lambda_block, flag_block, norm_scale, center, depths, first_pol)
        return totals + jnp.dot(block, phase_table, preferred_element_type=jnp.float32)

    start_totals = jnp.zeros((row_count, 2 * NPHI), jnp.float32)
    return lax.fori_loop(0, block_count, add_block, start_totals)


def depth_mask(row_counts):
    depth_ids = jnp.arange(NPHI, dtype=jnp.int32)
    middle = NPHI // 2
    lower = middle - DEPTH_BLOCK * row_counts
    upper = middle + DEPTH_BLOCK * row_counts
    inside = (depth_ids[None, :] >= lower[:, None]) & (depth_ids[None, :] < upper[:, None])
    return jnp.concatenate([inside, inside], 1)


def shards(stokes, lambda_sq, channel_flags, counts):
    local_stokes = stokes[0]
    flag_float = channel_flags.astype(jnp.float32)
    flag_total = jnp.sum(flag_float)
    norm_scale = 1.0 / jnp.sqrt(flag_total)
    center = jnp.sum(flag_float * lambda_sq) / flag_total
    first_pol = lax.axis_index("pol") == 0
    beam_count = lax.axis_size("beam")
    slab_count = lax.axis_size("slab")
    total_beams = counts.shape[0]
    pieces = 1
    piece_index = lax.axis_index("beam")
    piece_rows = total_beams // (beam_count * pieces)
    beam_ids = jnp.arange(total_beams, dtype=jnp.int32)
    row_ids = lax.dynamic_slice_in_dim(beam_ids, piece_index * piece_rows, piece_rows, 0)
    turned = lax.all_to_all(local_stokes, "beam", split_axis=0, concat_axis=1, tiled=True)
    slab_index = lax.axis_index("slab")
    lambda_local = lax.dynamic_index_in_dim(
        lambda_sq.reshape(beam_count, slab_count, -1), slab_index, 1, keepdims=False
    ).reshape(-1)
    flag_local = lax.dynamic_index_in_dim(
        flag_float.reshape(beam_count, slab_count, -1), slab_index, 1, keepdims=False
    ).reshape(-1)
    row_counts = jnp.take(counts, row_ids)
    partial_value = synth_dense(turned, lambda_local, flag_local, norm_scale, center, first_pol)
    partial_value = jnp.where(depth_mask(row_counts), partial_value, jnp.zeros_like(partial_value))
    spectrum = lax.psum_scatter(partial_value, ("slab", "pol"), scatter_dimension=0, tiled=True)
    return spectrum


def solution(mesh):
    in_specs = (P("pol", "grp", ("beam", "slab")), P(), P(), P("grp"))
    out_specs = P(("grp", "beam", "slab", "pol"), None)
    return jax.shard_map(shards, mesh=mesh, in_specs=in_specs, out_specs=out_specs, check_vma=False)
```

profile of v0, /device:TPU:0, one launch (start us, length us, event | category | flops | bytes accessed | tf_op | source)
XLA Modules:
  0.0 258.0 jit_solution(15316803507847317274)
XLA Ops:
  6.5 0.0 copy-start
  6.5 0.0 copy-start.1
  6.5 0.0 copy-start.2
  6.5 6.4 %all-to-all-start = ((bf16[4,128,2048]{2,1,0:T(8,128)(2,1)}), bf16[4,128,2048]{2,1,0:T(8,128)(2,1)S(1)}, u32[]{:S(2)}, u32[]{:S(2)}) async-start(bf16[4,128,2048]{2,1,0:T(8,128)(2,1)} %bitcast.6), calls=%async_computation | async-start | bytes 4194304 | tf_op jit(solution)/shard_map/all_to_all | solution.py:69
  13.0 0.0 reduce-scatter.2.cloned.1.call-start
  13.0 0.0 copy-done.1
  13.0 0.0 copy-done.2
  13.1 0.7 multiply_reduce_fusion
  15.9 0.1 compare_select_fusion
  15.9 0.0 copy-done
  15.9 1.3 gather_fusion
  17.2 0.1 broadcast_subtract_fusion
  17.3 0.1 constant_dynamic-slice_fusion
  17.4 0.2 fusion.19
  17.6 43.6 %all-to-all-done = bf16[4,128,2048]{2,1,0:T(8,128)(2,1)S(1)} async-done(((bf16[4,128,2048]{2,1,0:T(8,128)(2,1)}), bf16[4,128,2048]{2,1,0:T(8,128)(2,1)S(1)}, u32[]{:S(2)}, u32[]{:S(2)}) %all-to-all-start) | async-done | bytes 2097184 | tf_op jit(solution)/shard_map/all_to_all | solution.py:69
  61.2 2.5 copy.7
  63.7 162.2 %while.14 = (s32[]{:T(128)}, f32[128,2048]{1,0:T(8,128)S(1)}, bf16[128,8192]{0,1:T(8,128)(2,1)}, pred[]{:T(512)}, f32[]{:T(128)}, /*index=5*/f32[8192]{0:T(1024)...) while((s32[]{:T(128)}, f32[128,2048]{1,0:T(8,128)S(1)}, ...), condition=%wide.region_3.4_spmd.clone, body=%wide.region_2.3_spmd.clone.sunk | while | flops 554177536 | bytes 10780902 | solution.py:42
  63.7 17.7 %fusion.28 = (bf16[1024,1024]{1,0:T(8,128)(2,1)S(1)}, bf16[1024,1024]{1,0:T(8,128)(2,1)}) fusion(f32[1024]{0:T(1024)S(1)} %get-tuple-element.276, f32[1024]{0:T(1024)S(1)} %add_multiply_fusion.2, f32[1024]{0:T(1024)S(1)} %get-tuple-element.277, pred[]{:T(512)} %get-tuple-element.311), kind=kLoop, calls=%fused_computation.7.clone.1 | loop fusion | flops 8388608 | bytes 4206593 | tf_op jit(solution)/shard_map/while/body/eval_jaxpr/convert_element_type | solution.py:22
  81.4 2.5 fusion.29
  84.0 17.7 %fusion.28 = (bf16[1024,1024]{1,0:T(8,128)(2,1)S(1)}, bf16[1024,1024]{1,0:T(8,128)(2,1)}) fusion(f32[1024]{0:T(1024)S(1)} %get-tuple-element.276, f32[1024]{0:T(1024)S(1)} %add_multiply_fusion.2, f32[1024]{0:T(1024)S(1)} %get-tuple-element.277, pred[]{:T(512)} %get-tuple-element.311), kind=kLoop, calls=%fused_computation.7.clone.1 | loop fusion | flops 8388608 | bytes 4206593 | tf_op jit(solution)/shard_map/while/body/eval_jaxpr/convert_element_type | solution.py:22
  101.7 2.5 fusion.29
  104.3 17.7 %fusion.28 = (bf16[1024,1024]{1,0:T(8,128)(2,1)S(1)}, bf16[1024,1024]{1,0:T(8,128)(2,1)}) fusion(f32[1024]{0:T(1024)S(1)} %get-tuple-element.276, f32[1024]{0:T(1024)S(1)} %add_multiply_fusion.2, f32[1024]{0:T(1024)S(1)} %get-tuple-element.277, pred[]{:T(512)} %get-tuple-element.311), kind=kLoop, calls=%fused_computation.7.clone.1 | loop fusion | flops 8388608 | bytes 4206593 | tf_op jit(solution)/shard_map/while/body/eval_jaxpr/convert_element_type | solution.py:22
  122.0 2.5 fusion.29
  124.5 17.7 %fusion.28 = (bf16[1024,1024]{1,0:T(8,128)(2,1)S(1)}, bf16[1024,1024]{1,0:T(8,128)(2,1)}) fusion(f32[1024]{0:T(1024)S(1)} %get-tuple-element.276, f32[1024]{0:T(1024)S(1)} %add_multiply_fusion.2, f32[1024]{0:T(1024)S(1)} %get-tuple-element.277, pred[]{:T(512)} %get-tuple-element.311), kind=kLoop, calls=%fused_computation.7.clone.1 | loop fusion | flops 8388608 | bytes 4206593 | tf_op jit(solution)/shard_map/while/body/eval_jaxpr/convert_element_type | solution.py:22
  142.2 2.5 fusion.29
  144.8 17.7 %fusion.28 = (bf16[1024,1024]{1,0:T(8,128)(2,1)S(1)}, bf16[1024,1024]{1,0:T(8,128)(2,1)}) fusion(f32[1024]{0:T(1024)S(1)} %get-tuple-element.276, f32[1024]{0:T(1024)S(1)} %add_multiply_fusion.2, f32[1024]{0:T(1024)S(1)} %get-tuple-element.277, pred[]{:T(512)} %get-tuple-element.311), kind=kLoop, calls=%fused_computation.7.clone.1 | loop fusion | flops 8388608 | bytes 4206593 | tf_op jit(solution)/shard_map/while/body/eval_jaxpr/convert_element_type | solution.py:22
  162.5 2.5 fusion.29
  165.1 17.7 %fusion.28 = (bf16[1024,1024]{1,0:T(8,128)(2,1)S(1)}, bf16[1024,1024]{1,0:T(8,128)(2,1)}) fusion(f32[1024]{0:T(1024)S(1)} %get-tuple-element.276, f32[1024]{0:T(1024)S(1)} %add_multiply_fusion.2, f32[1024]{0:T(1024)S(1)} %get-tuple-element.277, pred[]{:T(512)} %get-tuple-element.311), kind=kLoop, calls=%fused_computation.7.clone.1 | loop fusion | flops 8388608 | bytes 4206593 | tf_op jit(solution)/shard_map/while/body/eval_jaxpr/convert_element_type | solution.py:22
  182.8 2.5 fusion.29
  185.4 17.7 %fusion.28 = (bf16[1024,1024]{1,0:T(8,128)(2,1)S(1)}, bf16[1024,1024]{1,0:T(8,128)(2,1)}) fusion(f32[1024]{0:T(1024)S(1)} %get-tuple-element.276, f32[1024]{0:T(1024)S(1)} %add_multiply_fusion.2, f32[1024]{0:T(1024)S(1)} %get-tuple-element.277, pred[]{:T(512)} %get-tuple-element.311), kind=kLoop, calls=%fused_computation.7.clone.1 | loop fusion | flops 8388608 | bytes 4206593 | tf_op jit(solution)/shard_map/while/body/eval_jaxpr/convert_element_type | solution.py:22
  203.1 2.5 fusion.29
  205.7 17.7 %fusion.28 = (bf16[1024,1024]{1,0:T(8,128)(2,1)S(1)}, bf16[1024,1024]{1,0:T(8,128)(2,1)}) fusion(f32[1024]{0:T(1024)S(1)} %get-tuple-element.276, f32[1024]{0:T(1024)S(1)} %add_multiply_fusion.2, f32[1024]{0:T(1024)S(1)} %get-tuple-element.277, pred[]{:T(512)} %get-tuple-element.311), kind=kLoop, calls=%fused_computation.7.clone.1 | loop fusion | flops 8388608 | bytes 4206593 | tf_op jit(solution)/shard_map/while/body/eval_jaxpr/convert_element_type | solution.py:22
  223.4 2.5 fusion.29
  225.9 1.1 add_select_fusion
  227.0 0.0 reduce-scatter.2.cloned.1.call-update
  227.0 24.2 %reduce-scatter.2.cloned.1.call-done = f32[32,2048]{1,0:T(8,128)} async-done(((f32[128,2048]{1,0:T(8,128)}), f32[32,2048]{1,0:T(8,128)}) %reduce-scatter.2.cloned.1.call-update) | async-done | bytes 262160 | tf_op jit(solution)/shard_map/reduce_scatter | solution.py:80
  (23 shorter events, 0.2 us)
Async XLA Ops:
  6.5 9.4 %copy-start = (s32[512]{0:T(512)S(1)}, s32[512]{0:T(512)}, u32[]{:S(2)}) copy-start(s32[512]{0:T(512)} %param.9) | copy-start | bytes 6148
  6.5 6.5 %copy-start.1 = (f32[16384]{0:T(1024)S(1)}, f32[16384]{0:T(1024)}, u32[]{:S(2)}) copy-start(f32[16384]{0:T(1024)} %param.7) | copy-start | bytes 196612
  6.5 6.5 %copy-start.2 = (s32[16384]{0:T(1024)S(1)}, s32[16384]{0:T(1024)}, u32[]{:S(2)}) copy-start(s32[16384]{0:T(1024)} %param.8) | copy-start | bytes 196612
  6.5 54.6 %all-to-all-start = ((bf16[4,128,2048]{2,1,0:T(8,128)(2,1)}), bf16[4,128,2048]{2,1,0:T(8,128)(2,1)S(1)}, u32[]{:S(2)}, u32[]{:S(2)}) async-start(bf16[4,128,2048]{2,1,0:T(8,128)(2,1)} %bitcast.6), calls=%async_computation | async-start | bytes 4194304 | tf_op jit(solution)/shard_map/all_to_all | solution.py:69
  13.0 238.2 %reduce-scatter.2.cloned.1.call-start = ((), (), s32[]{:S(2)}) async-start(), calls=%async_computation.2 | async-start | bytes 1310720 | tf_op jit(solution)/shard_map/reduce_scatter | solution.py:80
Sparse Core Ops, SparseCore 0:
  227.1 23.9 reduce-scatter.1
where the time goes:
time: 259 us; the launch traced here: 258 us
  other arithmetic  144 us (56%)
  waiting for transfers between devices  67.7 us (26%)
  matrix products  20.1 us (8%)
  between operations  15.5 us (6%)
  starting transfers between devices  6.45 us (2%)
  local copies, waits for them, and re-layouts  3.92 us (2%)
    convert_element_type x8, other arithmetic, build_table(): first_table = jnp.where(first_pol, cos_part, sin_part).astype(jnp.bfloat16)  142 us
    all_to_all x1, waiting for transfers between devices, shards(): lax.all_to_all(local_stokes, 'beam', split_axis=0, concat_axis=1, tiled=T...  43.6 us
    reduce_scatter x1, waiting for transfers between devices, shards(): lax.psum_scatter(partial_value, ('slab', 'pol'), scatter_dimension=0, til...  24.2 us
    dot_general x8, matrix products, add_block(): jnp.dot(block, phase_table, preferred_element_type=jnp.float32)  20.1 us
    all_to_all x1, starting transfers between devices, shards(): lax.all_to_all(local_stokes, 'beam', split_axis=0, concat_axis=1, tiled=T...  6.45 us
  transfers between devices with their start and end apart: 2, of which 2 were waited for; matrix products, arithmetic and copies ran while one was open for 1% of the time, Pallas kernels for 0%

commit v1 on v0

--- a/solution.py
+++ b/solution.py
@@ -1,10 +1,16 @@
+import functools
+import math
+
 import jax
 import jax.numpy as jnp
 from jax import lax
+from jax.experimental import pallas as pl
+from jax.experimental.pallas import tpu as pltpu
 from jax.sharding import PartitionSpec as P
 
 NPHI = 1024
 DEPTH_BLOCK = 128
+MESH = pl.DeviceIdType.MESH
 
 
 depth_step = 32.0
@@ -51,7 +57,7 @@
     return jnp.concatenate([inside, inside], 1)
 
 
-def shards(stokes, lambda_sq, channel_flags, counts):
+def general_shards(stokes, lambda_sq, channel_flags, counts):
     local_stokes = stokes[0]
     flag_float = channel_flags.astype(jnp.float32)
     flag_total = jnp.sum(flag_float)
@@ -61,11 +67,8 @@
     beam_count = lax.axis_size("beam")
     slab_count = lax.axis_size("slab")
     total_beams = counts.shape[0]
-    pieces = 1
     piece_index = lax.axis_index("beam")
-    piece_rows = total_beams // (beam_count * pieces)
-    beam_ids = jnp.arange(total_beams, dtype=jnp.int32)
-    row_ids = lax.dynamic_slice_in_dim(beam_ids, piece_index * piece_rows, piece_rows, 0)
+    piece_rows = total_beams // beam_count
     turned = lax.all_to_all(local_stokes, "beam", split_axis=0, concat_axis=1, tiled=True)
     slab_index = lax.axis_index("slab")
     lambda_local = lax.dynamic_index_in_dim(
@@ -74,14 +77,305 @@
     flag_local = lax.dynamic_index_in_dim(
         flag_float.reshape(beam_count, slab_count, -1), slab_index, 1, keepdims=False
     ).reshape(-1)
-    row_counts = jnp.take(counts, row_ids)
+    row_counts = lax.dynamic_slice_in_dim(counts, piece_index * piece_rows, piece_rows, 0)
     partial_value = synth_dense(turned, lambda_local, flag_local, norm_scale, center, first_pol)
     partial_value = jnp.where(depth_mask(row_counts), partial_value, jnp.zeros_like(partial_value))
-    spectrum = lax.psum_scatter(partial_value, ("slab", "pol"), scatter_dimension=0, tiled=True)
-    return spectrum
+    return lax.psum_scatter(partial_value, ("slab", "pol"), scatter_dimension=0, tiled=True)
+
+
+LANES = 128
+PORTIONS = 4
+COLS = NPHI // PORTIONS
+FINE = 64
+COARSE = NPHI // FINE
+
+HALF_TURN_HI = 3.140625
+HALF_TURN_MID = 9.670257568359375e-04
+HALF_TURN_LO = math.pi - HALF_TURN_HI - HALF_TURN_MID
+
+
+def cos_sin(phase):
+    turns = jnp.floor(phase * (1.0 / math.pi) + 0.5)
+    rest = phase - turns * HALF_TURN_HI
+    rest = rest - turns * HALF_TURN_MID
+    rest = rest - turns * HALF_TURN_LO
+    sign = 1.0 - 2.0 * (turns - 2.0 * jnp.floor(turns * 0.5))
+    square = rest * rest
+    cos_sum = jnp.full_like(square, 1.0 / math.factorial(12))
+    for order in (10, 8, 6, 4, 2, 0):
+        cos_sum = cos_sum * square + (-1.0) ** (order // 2) / math.factorial(order)
+    sin_sum = jnp.full_like(square, -1.0 / math.factorial(11))
+    for order in (9, 7, 5, 3, 1):
+        sin_sum = sin_sum * square + (-1.0) ** (order // 2) / math.factorial(order)
+    return sign * cos_sum, sign * rest * sin_sum
+
+
+def kernel(nz, nx, rows, chans,
+           stokes_ref, lam_ref, flag_ref, out_ref,
+           data, fine, coarse, table, sums, xout, xin, zout, zin,
+           local_sem, pol_send, pol_recv, x_send, x_recv, z_send, z_recv):
+    z = lax.axis_index("beam")
+    x = lax.axis_index("slab")
+    p = lax.axis_index("pol")
+    groups = chans // LANES
+
+    barrier = pltpu.get_barrier_semaphore()
+    pl.semaphore_signal(barrier, inc=1, device_id={"pol": 1 - p}, device_id_type=MESH)
+    pl.semaphore_signal(barrier, inc=1, device_id={"slab": 1 - x}, device_id_type=MESH)
+
+    @pl.when(z > 0)
+    def _():
+        pl.semaphore_signal(barrier, inc=1, device_id={"beam": z - 1}, device_id_type=MESH)
+
+    @pl.when(z < nz - 1)
+    def _():
+        pl.semaphore_signal(barrier, inc=1, device_id={"beam": z + 1}, device_id_type=MESH)
+
+    def local_copy(xd):
+        return pltpu.make_async_copy(stokes_ref.at[:, xd, p], data.at[0, xd], local_sem.at[xd])
+
+    def pol_copy(xd):
+        return pltpu.make_async_remote_copy(
+            src_ref=stokes_ref.at[:, xd, 1 - p], dst_ref=data.at[1, xd],
+            send_sem=pol_send.at[xd], recv_sem=pol_recv.at[xd],
+            device_id={"pol": 1 - p}, device_id_type=MESH)
+
+    def x_copy(j):
+        return pltpu.make_async_remote_copy(
+            src_ref=xout.at[j], dst_ref=xin.at[j],
+            send_sem=x_send.at[j], recv_sem=x_recv.at[j],
+            device_id={"slab": 1 - x}, device_id_type=MESH)
+
+    def z_copy(j, d, way):
+        return pltpu.make_async_remote_copy(
+            src_ref=zout.at[j, d], dst_ref=zin.at[j, d, way],
+            send_sem=z_send.at[j, d], recv_sem=z_recv.at[j, d, way],
+            device_id={"beam": z + 1 - 2 * way}, device_id_type=MESH)
+
+    for xd in range(nx):
+        local_copy(xd).start()
+
+    at_end = (z == 0) | (z == nz - 1)
+
+    @pl.when(at_end)
+    def _():
+        pl.semaphore_wait(barrier, 3)
+
+    @pl.when(jnp.logical_not(at_end))
+    def _():
+        pl.semaphore_wait(barrier, 4)
+
+    for xd in range(nx):
+        pol_copy(xd).start()
+
+    flags = flag_ref[...].astype(jnp.float32)
+    flag_total = jnp.sum(jnp.sum(flags, 0, keepdims=True), 1, keepdims=True)
+    lam_total = jnp.sum(jnp.sum(flags * lam_ref[...], 0, keepdims=True), 1, keepdims=True)
+    norm_scale = 1.0 / jnp.sqrt(flag_total)
+    center = lam_total / flag_total
+    first_group = (z * nx + x) * groups
+    row_id = lax.broadcasted_iota(jnp.int32, (8, LANES), 0).astype(jnp.float32)
+    step = 2.0 * depth_step
+
+    def factors(g, carry):
+        lanes = pl.ds(pl.multiple_of(g * LANES, LANES), LANES)
+        offset = lam_ref[pl.ds(first_group + g, 1), :] - center
+        weight = norm_scale * flag_ref[pl.ds(first_group + g, 1), :].astype(jnp.float32)
+        cos_c, sin_c = cos_sin((step * row_id) * offset)
+        cos_b, sin_b = cos_sin((step * 8.0 * row_id) * offset)
+        for b in range(8):
+            cb, sb = cos_b[b:b + 1, :], sin_b[b:b + 1, :]
+            fine[0, b * 8:b * 8 + 8, lanes] = cb * cos_c - sb * sin_c
+            fine[1, b * 8:b * 8 + 8, lanes] = sb * cos_c + cb * sin_c
+        for half in range(COARSE // 8):
+            ca, sa = cos_sin((step * FINE * (row_id + (8.0 * half - COARSE // 2))) * offset)
+            coarse[0, half * 8:half * 8 + 8, lanes] = ca * weight
+            coarse[1, half * 8:half * 8 + 8, lanes] = sa * weight
+        return carry
+
+    lax.fori_loop(0, groups, factors, 0)
+
+    for xd in range(nx):
+        local_copy(xd).wait()
+        pol_copy(xd).wait()
+
+    width = 256
+
+    def compute(j):
+        def fill(i, carry):
+            a = i // (chans // width)
+            lanes = pl.ds(pl.multiple_of((i % (chans // width)) * width, width), width)
+            out_rows = pl.ds(pl.multiple_of(a * FINE, FINE), FINE)
+            ca = coarse[0, pl.ds(j * (COLS // FINE) + a, 1), lanes]
+            sa = coarse[1, pl.ds(j * (COLS // FINE) + a, 1), lanes]
+            cf = fine[0, :, lanes]
+            sf = fine[1, :, lanes]
+            table[p, out_rows, lanes] = (ca * cf - sa * sf).astype(jnp.bfloat16)
+            table[1 - p, out_rows, lanes] = (sa * cf + ca * sf).astype(jnp.bfloat16)
+            return carry
+
+        lax.fori_loop(0, (COLS // FINE) * (chans // width), fill, 0)
+        sign = 1.0 - 2.0 * p.astype(jnp.float32)
+        dims = (((1,), (1,)), ((), ()))
+        half_rows = nz * rows
+
+        def half(i, carry):
+            xd = lax.rem(1 - x + i + nx, nx)
+            both = data[:, xd].reshape(2 * half_rows, chans)
+            first = lax.dot_general(both, table[0], dims, preferred_element_type=jnp.float32)
+            second = lax.dot_general(both, table[1], dims, preferred_element_type=jnp.float32)
+            real = first[:half_rows] + second[half_rows:]
+            imag = sign * (first[half_rows:] - second[:half_rows])
+
+            @pl.when(i == 0)
+            def _():
+                xout[j, 0] = real.astype(jnp.bfloat16)
+                xout[j, 1] = imag.astype(jnp.bfloat16)
+                x_copy(j).start()
+
+            @pl.when(i == 1)
+            def _():
+                sums[j, 0] = real
+                sums[j, 1] = imag
+
+            return carry
+
+        lax.fori_loop(0, nx, half, 0)
+
+    def block(d):
+        return slice(d * rows, d * rows + rows)
+
+    def send(j, d, way, came):
+        value = sums[j, :, block(d), :]
+        if came:
+            value = value + zin[j, d, way].astype(jnp.float32)
+        zout[j, d] = value.astype(jnp.bfloat16)
+        z_copy(j, d, way).start()
+
+    def after_x(j):
+        x_copy(j).wait_recv()
+        sums[j] = sums[j] + xin[j].astype(jnp.float32)
+
+        @pl.when(z == 0)
+        def _():
+            for d in range(nz - 1, 0, -1):
+                send(j, d, 0, False)
+
+        @pl.when(z == nz - 1)
+        def _():
+            for d in range(nz - 1):
+                send(j, d, 1, False)
+
+    def hop(j, h):
+        for d in range(nz - 1, h, -1):
+            @pl.when(z == h)
+            def _():
+                z_copy(j, d, 0).wait_recv()
+                send(j, d, 0, True)
+
+        for d in range(nz - 1 - h):
+            @pl.when(z == nz - 1 - h)
+            def _():
+                z_copy(j, d, 1).wait_recv()
+                send(j, d, 1, True)
+
+    def finish(j):
+        for d in range(nz):
+            @pl.when(z == d)
+            def _():
+                value = sums[j, :, block(d), :]
+                if d > 0:
+                    z_copy(j, d, 0).wait_recv()
+                    value = value + zin[j, d, 0].astype(jnp.float32)
+                if d < nz - 1:
+                    z_copy(j, d, 1).wait_recv()
+                    value = value + zin[j, d, 1].astype(jnp.float32)
+                for part in range(2):
+                    columns = pl.ds(pl.multiple_of(part * NPHI + j * COLS, COLS), COLS)
+                    out_ref[:, columns] = value[part]
+
+    def stage(i, carry):
+        @pl.when(i < PORTIONS)
+        def _():
+            compute(i)
+
+        def late(lag, action):
+            @pl.when((i >= lag) & (i < PORTIONS + lag))
+            def _():
+                action(i - lag)
+
+        late(1, after_x)
+        for h in range(1, nz - 1):
+            late(1 + h, lambda j, h=h: hop(j, h))
+        late(nz, finish)
+        return carry
+
+    lax.fori_loop(0, PORTIONS + nz, stage, 0)
+
+    def drain(j, carry):
+        x_copy(j).wait_send()
+        for d in range(nz):
+            @pl.when(z < d)
+            def _():
+                z_copy(j, d, 0).wait_send()
+
+            @pl.when(z > d)
+            def _():
+                z_copy(j, d, 1).wait_send()
+        return carry
+
+    lax.fori_loop(0, PORTIONS, drain, 0)
+
+
+def kernel_shards(nz, nx, stokes, lambda_sq, channel_flags, counts):
+    beams = counts.shape[0]
+    chans = stokes.shape[2]
+    rows = beams // (nz * nx * 2)
+    bf16, f32 = jnp.bfloat16, jnp.float32
+    DMA = pltpu.SemaphoreType.DMA
+    spectrum = pl.pallas_call(
+        functools.partial(kernel, nz, nx, rows, chans),
+        out_shape=jax.ShapeDtypeStruct((rows, 2 * NPHI), f32),
+        in_specs=[
+            pl.BlockSpec(memory_space=pl.ANY),
+            pl.BlockSpec(memory_space=pltpu.VMEM),
+            pl.BlockSpec(memory_space=pltpu.VMEM),
+        ],
+        out_specs=pl.BlockSpec(memory_space=pltpu.VMEM),
+        scratch_shapes=[
+            pltpu.VMEM((2, nx, nz, rows, chans), bf16),
+            pltpu.VMEM((2, FINE, chans), f32),
+            pltpu.VMEM((2, COARSE, chans), f32),
+            pltpu.VMEM((2, COLS, chans), bf16),
+            pltpu.VMEM((PORTIONS, 2, nz * rows, COLS), f32),
+            pltpu.VMEM((PORTIONS, 2, nz * rows, COLS), bf16),
+            pltpu.VMEM((PORTIONS, 2, nz * rows, COLS), bf16),
+            pltpu.VMEM((PORTIONS, nz, 2, rows, COLS), bf16),
+            pltpu.VMEM((PORTIONS, nz, 2, 2, rows, COLS), bf16),
+            DMA((nx,)), DMA((nx,)), DMA((nx,)),
+            DMA((PORTIONS,)), DMA((PORTIONS,)),
+            DMA((PORTIONS, nz)), DMA((PORTIONS, nz, 2)),
+        ],
+        compiler_params=pltpu.CompilerParams(
+            collective_id=0, has_side_effects=True, vmem_limit_bytes=40 * 2**20),
+        cost_estimate=pl.CostEstimate(
+            flops=4 * beams * chans * NPHI, bytes_accessed=2 * beams * chans, transcendentals=0),
+    )(
+        stokes.reshape(nz, nx, 2, rows, chans),
+        lambda_sq.reshape(-1, LANES),
+        channel_flags.reshape(-1, LANES),
+    )
+    owner = (lax.axis_index("beam") * nx + lax.axis_index("slab")) * 2 + lax.axis_index("pol")
+    row_counts = lax.dynamic_slice_in_dim(counts, owner * rows, rows, 0)
+    return jnp.where(depth_mask(row_counts), spectrum, jnp.zeros_like(spectrum))
 
 
 def solution(mesh):
     in_specs = (P("pol", "grp", ("beam", "slab")), P(), P(), P("grp"))
     out_specs = P(("grp", "beam", "slab", "pol"), None)
-    return jax.shard_map(shards, mesh=mesh, in_specs=in_specs, out_specs=out_specs, check_vma=False)
+    nz, nx = mesh.shape["beam"], mesh.shape["slab"]
+    if nx == 2 and 2 <= nz <= 4 and mesh.shape["pol"] == 2:
+        body = functools.partial(kernel_shards, nz, nx)
+    else:
+        body = general_shards
+    return jax.shard_map(body, mesh=mesh, in_specs=in_specs, out_specs=out_specs, check_vma=False)

time: 259 us -> 37.3 us (0.14)
  other arithmetic: 144 us -> 1.58 us
  waiting for transfers between devices: 67.7 us -> 0 us
  Pallas kernels: 0 us -> 32.1 us
  matrix products: 20.1 us -> 0 us
  between operations: 15.5 us -> 0.03 us
  starting transfers between devices: 6.45 us -> 0 us
    convert_element_type x9 -> x0, other arithmetic: 142 us -> none  [the longest x8 142 us: build_table(): first_table = jnp.where(first_pol, cos_part, sin_part).astype(jnp.bfloat16)]
    all_to_all x1 -> x0, waiting for transfers between devices: 43.6 us -> none  [shards(): lax.all_to_all(local_stokes, 'beam', split_axis=0, concat_axis=1, tiled=T...]
    pallas_call x0 -> x1, Pallas kernels: none -> 32.1 us  [kernel_shards(): pl.pallas_call(functools.partial(kernel, nz, nx, rows, chans), out_shape=...]
    reduce_scatter x1 -> x0, waiting for transfers between devices: 24.2 us -> none  [shards(): lax.psum_scatter(partial_value, ('slab', 'pol'), scatter_dimension=0, til...]
    dot_general x8 -> x0, matrix products: 20.1 us -> none  [add_block(): jnp.dot(block, phase_table, preferred_element_type=jnp.float32)]
    all_to_all x1 -> x0, starting transfers between devices: 6.45 us -> none  [shards(): lax.all_to_all(local_stokes, 'beam', split_axis=0, concat_axis=1, tiled=T...]
    unnamed x6, local copies, waits for them, and re-layouts: 0.01 us -> 3.26 us
  transfers between devices with their start and end apart: 2 -> 0, of which waited for: 2 -> 0; matrix products, arithmetic and copies ran while one was open for 1% -> 0% of each run, Pallas kernels for 0% -> 0%
where the time goes in v1:
time: 37.3 us; the launch traced here: 37 us
  Pallas kernels  32.1 us (86%)
  local copies, waits for them, and re-layouts  3.26 us (9%)
  other arithmetic  1.58 us (4%)
    pallas_call x1, Pallas kernels, kernel_shards(): pl.pallas_call(functools.partial(kernel, nz, nx, rows, chans), out_shape=...  32.1 us
    unnamed x6, local copies, waits for them, and re-layouts  3.26 us
    sub x1, other arithmetic, depth_mask(): lower = middle - DEPTH_BLOCK * row_counts  0.76 us

profile of v1, /device:TPU:0, one launch (start us, length us, event | category | flops | bytes accessed | tf_op | source)
XLA Modules:
  0.0 37.0 jit_solution(928197332219538235)
XLA Ops:
  0.0 0.8 %broadcast_subtract_fusion = (s32[32]{0:T(128)S(1)}, s32[32]{0:T(128)S(1)}) fusion(s32[512]{0:T(512)} %param.7, s32[]{:T(128)S(6)} %select_n.7), kind=kLoop, calls=%fused_computation.6 | loop fusion | flops 96 | bytes 388 | tf_op jit(solution)/shard_map/sub | solution.py:54
  0.8 0.1 fusion
  0.9 0.0 copy-start
  0.9 1.6 %copy-done = bf16[1,512,2048]{2,1,0:T(8,128)(2,1)S(1)} copy-done((bf16[1,512,2048]{2,1,0:T(8,128)(2,1)S(1)}, bf16[1,512,2048]{2,1,0:T(8,128)(2,1)}, u32[]{:S(2)}) %copy-start) | copy-done | bytes 2097176
  2.5 0.0 copy-start.1
  2.5 0.8 %copy-done.1 = f32[16384]{0:T(1024)S(1)} copy-done((f32[16384]{0:T(1024)S(1)}, f32[16384]{0:T(1024)}, u32[]{:S(2)}) %copy-start.1) | copy-done | bytes 65560
  3.3 0.0 copy-start.2
  3.3 0.8 %copy-done.2 = s32[16384]{0:T(1024)S(1)} copy-done((s32[16384]{0:T(1024)S(1)}, s32[16384]{0:T(1024)}, u32[]{:S(2)}) %copy-start.2) | copy-done | bytes 65560
  4.1 32.1 %shard_map.46 = f32[32,2048]{1,0:T(8,128)S(1)} custom-call(bf16[4,2,2,32,2048]{4,3,2,1,0:T(8,128)(2,1)S(1)} %bitcast.3, f32[128,128]{1,0:T(8,128)S(1)} %bitcast.4, s32[128,128]{1,0:T(8,128)S(1)} %bitcast.5), custom_call_target="tpu_custom_call" | custom-call | flops 4294967296 | bytes 2097152 | tf_op jit(solution)/shard_map/pallas_call | solution.py:336
  36.3 0.7 %add_select_fusion = f32[32,2048]{1,0:T(8,128)} fusion(f32[32,2048]{1,0:T(8,128)S(1)} %shard_map.46, pred[32,1024]{1,0:T(8,128)(4,1)S(1)} %fusion), kind=kLoop, calls=%fused_computation | loop fusion | flops 131072 | bytes 557056 | tf_op jit(solution)/shard_map/jit(_where)/select_n | solution.py:370
Async XLA Ops:
  0.9 1.6 %copy-start = (bf16[1,512,2048]{2,1,0:T(8,128)(2,1)S(1)}, bf16[1,512,2048]{2,1,0:T(8,128)(2,1)}, u32[]{:S(2)}) copy-start(bf16[1,512,2048]{2,1,0:T(8,128)(2,1)} %param.4) | copy-start | bytes 6291460
  2.5 0.8 %copy-start.1 = (f32[16384]{0:T(1024)S(1)}, f32[16384]{0:T(1024)}, u32[]{:S(2)}) copy-start(f32[16384]{0:T(1024)} %param.5) | copy-start | bytes 196612
  3.3 0.8 %copy-start.2 = (s32[16384]{0:T(1024)S(1)}, s32[16384]{0:T(1024)}, u32[]{:S(2)}) copy-start(s32[16384]{0:T(1024)} %param.6) | copy-start | bytes 196612

commit v2 on v1

--- a/solution.py
+++ b/solution.py
@@ -89,6 +89,8 @@
 FINE = 64
 COARSE = NPHI // FINE
 
+VMEM_BYTES = 60 * 2**20
+
 HALF_TURN_HI = 3.140625
 HALF_TURN_MID = 9.670257568359375e-04
 HALF_TURN_LO = math.pi - HALF_TURN_HI - HALF_TURN_MID
@@ -111,25 +113,37 @@
 
 
 def kernel(nz, nx, rows, chans,
-           stokes_ref, lam_ref, flag_ref, out_ref,
+           stokes_ref, lam_hbm, flag_hbm, count_hbm, out_ref,
+           lam_ref, flag_ref, count_ref,
            data, fine, coarse, table, sums, xout, xin, zout, zin,
-           local_sem, pol_send, pol_recv, x_send, x_recv, z_send, z_recv):
+           small_sem, local_sem, pol_send, pol_recv, x_send, x_recv, z_send, z_recv):
     z = lax.axis_index("beam")
     x = lax.axis_index("slab")
     p = lax.axis_index("pol")
     groups = chans // LANES
 
+    side = z // 2
+    outer = (z == 0) | (z == nz - 1)
+    near_in, near_out = 1 + side, 3 * side
+    far_in, far_out = 2 - side, 3 - 3 * side
+
     barrier = pltpu.get_barrier_semaphore()
-    pl.semaphore_signal(barrier, inc=1, device_id={"pol": 1 - p}, device_id_type=MESH)
-    pl.semaphore_signal(barrier, inc=1, device_id={"slab": 1 - x}, device_id_type=MESH)
-
-    @pl.when(z > 0)
+
+    def greet(**device):
+        pl.semaphore_signal(barrier, inc=1, device_id=device, device_id_type=MESH)
+
+    greet(pol=1 - p)
+    greet(slab=1 - x)
+    greet(beam=far_in)
+
+    @pl.when(outer)
     def _():
-        pl.semaphore_signal(barrier, inc=1, device_id={"beam": z - 1}, device_id_type=MESH)
-
-    @pl.when(z < nz - 1)
+        greet(beam=near_in)
+
+    @pl.when(jnp.logical_not(outer))
     def _():
-        pl.semaphore_signal(barrier, inc=1, device_id={"beam": z + 1}, device_id_type=MESH)
+        greet(beam=near_out)
+        greet(beam=far_out)
 
     def local_copy(xd):
         return pltpu.make_async_copy(stokes_ref.at[:, xd, p], data.at[0, xd], local_sem.at[xd])
@@ -146,28 +160,32 @@
             send_sem=x_send.at[j], recv_sem=x_recv.at[j],
             device_id={"slab": 1 - x}, device_id_type=MESH)
 
-    def z_copy(j, d, way):
+    def z_copy(j, taken, slot, to):
         return pltpu.make_async_remote_copy(
-            src_ref=zout.at[j, d], dst_ref=zin.at[j, d, way],
-            send_sem=z_send.at[j, d], recv_sem=z_recv.at[j, d, way],
-            device_id={"beam": z + 1 - 2 * way}, device_id_type=MESH)
-
+            src_ref=zout.at[j, taken], dst_ref=zin.at[j, slot],
+            send_sem=z_send.at[j, taken], recv_sem=z_recv.at[j, slot],
+            device_id={"beam": to}, device_id_type=MESH)
+
+    small = [pltpu.make_async_copy(source, held, small_sem.at[i]) for i, (source, held) in enumerate(
+        [(lam_hbm, lam_ref), (flag_hbm, flag_ref), (count_hbm, count_ref)])]
+    for copy in small:
+        copy.start()
     for xd in range(nx):
         local_copy(xd).start()
 
-    at_end = (z == 0) | (z == nz - 1)
-
-    @pl.when(at_end)
-    def _():
-        pl.semaphore_wait(barrier, 3)
-
-    @pl.when(jnp.logical_not(at_end))
+    @pl.when(outer)
     def _():
         pl.semaphore_wait(barrier, 4)
 
+    @pl.when(jnp.logical_not(outer))
+    def _():
+        pl.semaphore_wait(barrier, 5)
+
     for xd in range(nx):
         pol_copy(xd).start()
 
+    for copy in small:
+        copy.wait()
     flags = flag_ref[...].astype(jnp.float32)
     flag_total = jnp.sum(jnp.sum(flags, 0, keepdims=True), 1, keepdims=True)
     lam_total = jnp.sum(jnp.sum(flags * lam_ref[...], 0, keepdims=True), 1, keepdims=True)
@@ -195,10 +213,6 @@
 
     lax.fori_loop(0, groups, factors, 0)
 
-    for xd in range(nx):
-        local_copy(xd).wait()
-        pol_copy(xd).wait()
-
     width = 256
 
     def compute(j):
@@ -215,6 +229,13 @@
             return carry
 
         lax.fori_loop(0, (COLS // FINE) * (chans // width), fill, 0)
+
+        @pl.when(j == 0)
+        def _():
+            for xd in range(nx):
+                local_copy(xd).wait()
+                pol_copy(xd).wait()
+
         sign = 1.0 - 2.0 * p.astype(jnp.float32)
         dims = (((1,), (1,)), ((), ()))
         half_rows = nz * rows
@@ -242,57 +263,52 @@
 
         lax.fori_loop(0, nx, half, 0)
 
-    def block(d):
-        return slice(d * rows, d * rows + rows)
-
-    def send(j, d, way, came):
-        value = sums[j, :, block(d), :]
-        if came:
-            value = value + zin[j, d, way].astype(jnp.float32)
-        zout[j, d] = value.astype(jnp.bfloat16)
-        z_copy(j, d, way).start()
+    def total(j, d):
+        return sums[j, :, pl.ds(pl.multiple_of(d * rows, rows), rows), :]
+
+    def send(j, taken, slot, to, value):
+        zout[j, taken] = value.astype(jnp.bfloat16)
+        z_copy(j, taken, slot, to).start()
+
+    def arrived(j, slot):
+        z_copy(j, 0, slot, far_in).wait_recv()
+        return zin[j, slot].astype(jnp.float32)
 
     def after_x(j):
         x_copy(j).wait_recv()
         sums[j] = sums[j] + xin[j].astype(jnp.float32)
 
-        @pl.when(z == 0)
-        def _():
-            for d in range(nz - 1, 0, -1):
-                send(j, d, 0, False)
-
-        @pl.when(z == nz - 1)
-        def _():
-            for d in range(nz - 1):
-                send(j, d, 1, False)
-
-    def hop(j, h):
-        for d in range(nz - 1, h, -1):
-            @pl.when(z == h)
-            def _():
-                z_copy(j, d, 0).wait_recv()
-                send(j, d, 0, True)
-
-        for d in range(nz - 1 - h):
-            @pl.when(z == nz - 1 - h)
-            def _():
-                z_copy(j, d, 1).wait_recv()
-                send(j, d, 1, True)
+        @pl.when(outer)
+        def _():
+            send(j, 0, 2, near_in, total(j, far_out))
+            send(j, 1, 1, near_in, total(j, far_in))
+            send(j, 2, 0, near_in, total(j, near_in))
+
+        @pl.when(jnp.logical_not(outer))
+        def _():
+            send(j, 0, 0, near_out, total(j, near_out))
+
+    def hop(j):
+        @pl.when(jnp.logical_not(outer))
+        def _():
+            send(j, 1, 3, far_out, total(j, far_out) + arrived(j, 2))
+            send(j, 2, 3, far_in, total(j, far_in) + arrived(j, 1))
 
     def finish(j):
-        for d in range(nz):
-            @pl.when(z == d)
-            def _():
-                value = sums[j, :, block(d), :]
-                if d > 0:
-                    z_copy(j, d, 0).wait_recv()
-                    value = value + zin[j, d, 0].astype(jnp.float32)
-                if d < nz - 1:
-                    z_copy(j, d, 1).wait_recv()
-                    value = value + zin[j, d, 1].astype(jnp.float32)
-                for part in range(2):
-                    columns = pl.ds(pl.multiple_of(part * NPHI + j * COLS, COLS), COLS)
-                    out_ref[:, columns] = value[part]
+        value = total(j, z) + arrived(j, 0) + arrived(j, 3)
+        depth_id = j * COLS + lax.broadcasted_iota(jnp.int32, (rows, COLS), 1)
+        inside = (depth_id >= NPHI // 2 - DEPTH_BLOCK * row_counts) & (
+            depth_id < NPHI // 2 + DEPTH_BLOCK * row_counts)
+        for part in range(2):
+            columns = pl.ds(pl.multiple_of(part * NPHI + j * COLS, COLS), COLS)
+            out_ref[:, columns] = jnp.where(inside, value[part], 0.0)
+
+    owner = (z * nx + x) * 2 + p
+    per_row = LANES // rows
+    count_row = jnp.broadcast_to(count_ref[pl.ds(owner // per_row, 1), :], (rows, LANES))
+    lane_id = lax.broadcasted_iota(jnp.int32, (rows, LANES), 1)
+    own_lane = lax.broadcasted_iota(jnp.int32, (rows, LANES), 0) + lax.rem(owner, per_row) * rows
+    row_counts = jnp.sum(jnp.where(lane_id == own_lane, count_row, 0), 1, keepdims=True)
 
     def stage(i, carry):
         @pl.when(i < PORTIONS)
@@ -305,23 +321,16 @@
                 action(i - lag)
 
         late(1, after_x)
-        for h in range(1, nz - 1):
-            late(1 + h, lambda j, h=h: hop(j, h))
-        late(nz, finish)
+        late(2, hop)
+        late(3, finish)
         return carry
 
-    lax.fori_loop(0, PORTIONS + nz, stage, 0)
+    lax.fori_loop(0, PORTIONS + 3, stage, 0)
 
     def drain(j, carry):
         x_copy(j).wait_send()
-        for d in range(nz):
-            @pl.when(z < d)
-            def _():
-                z_copy(j, d, 0).wait_send()
-
-            @pl.when(z > d)
-            def _():
-                z_copy(j, d, 1).wait_send()
+        for taken in range(3):
+            z_copy(j, taken, 0, far_in).wait_send()
         return carry
 
     lax.fori_loop(0, PORTIONS, drain, 0)
@@ -336,13 +345,12 @@
     spectrum = pl.pallas_call(
         functools.partial(kernel, nz, nx, rows, chans),
         out_shape=jax.ShapeDtypeStruct((rows, 2 * NPHI), f32),
-        in_specs=[
-            pl.BlockSpec(memory_space=pl.ANY),
-            pl.BlockSpec(memory_space=pltpu.VMEM),
-            pl.BlockSpec(memory_space=pltpu.VMEM),
-        ],
+        in_specs=[pl.BlockSpec(memory_space=pl.ANY)] * 4,
         out_specs=pl.BlockSpec(memory_space=pltpu.VMEM),
         scratch_shapes=[
+            pltpu.VMEM((lambda_sq.shape[0] // LANES, LANES), f32),
+            pltpu.VMEM((lambda_sq.shape[0] // LANES, LANES), jnp.int32),
+            pltpu.VMEM((beams // LANES, LANES), jnp.int32),
             pltpu.VMEM((2, nx, nz, rows, chans), bf16),
             pltpu.VMEM((2, FINE, chans), f32),
             pltpu.VMEM((2, COARSE, chans), f32),
@@ -350,31 +358,30 @@
             pltpu.VMEM((PORTIONS, 2, nz * rows, COLS), f32),
             pltpu.VMEM((PORTIONS, 2, nz * rows, COLS), bf16),
             pltpu.VMEM((PORTIONS, 2, nz * rows, COLS), bf16),
-            pltpu.VMEM((PORTIONS, nz, 2, rows, COLS), bf16),
-            pltpu.VMEM((PORTIONS, nz, 2, 2, rows, COLS), bf16),
-            DMA((nx,)), DMA((nx,)), DMA((nx,)),
+            pltpu.VMEM((PORTIONS, 3, 2, rows, COLS), bf16),
+            pltpu.VMEM((PORTIONS, 4, 2, rows, COLS), bf16),
+            DMA((3,)), DMA((nx,)), DMA((nx,)), DMA((nx,)),
             DMA((PORTIONS,)), DMA((PORTIONS,)),
-            DMA((PORTIONS, nz)), DMA((PORTIONS, nz, 2)),
+            DMA((PORTIONS, 3)), DMA((PORTIONS, 4)),
         ],
         compiler_params=pltpu.CompilerParams(
-            collective_id=0, has_side_effects=True, vmem_limit_bytes=40 * 2**20),
+            collective_id=0, has_side_effects=True, vmem_limit_bytes=VMEM_BYTES),
         cost_estimate=pl.CostEstimate(
             flops=4 * beams * chans * NPHI, bytes_accessed=2 * beams * chans, transcendentals=0),
     )(
         stokes.reshape(nz, nx, 2, rows, chans),
         lambda_sq.reshape(-1, LANES),
         channel_flags.reshape(-1, LANES),
+        counts.reshape(-1, LANES),
     )
-    owner = (lax.axis_index("beam") * nx + lax.axis_index("slab")) * 2 + lax.axis_index("pol")
-    row_counts = lax.dynamic_slice_in_dim(counts, owner * rows, rows, 0)
-    return jnp.where(depth_mask(row_counts), spectrum, jnp.zeros_like(spectrum))
+    return spectrum
 
 
 def solution(mesh):
     in_specs = (P("pol", "grp", ("beam", "slab")), P(), P(), P("grp"))
     out_specs = P(("grp", "beam", "slab", "pol"), None)
     nz, nx = mesh.shape["beam"], mesh.shape["slab"]
-    if nx == 2 and 2 <= nz <= 4 and mesh.shape["pol"] == 2:
+    if nx == 2 and nz == 4 and mesh.shape["pol"] == 2:
         body = functools.partial(kernel_shards, nz, nx)
     else:
         body = general_shards

time: 37.3 us -> 31.3 us (0.84)
  Pallas kernels: 32.1 us -> 29.5 us
  local copies, waits for them, and re-layouts: 3.26 us -> 1.67 us
  other arithmetic: 1.58 us -> 0 us
    pallas_call x1, Pallas kernels: 32.1 us -> 29.5 us  [kernel_shards(): pl.pallas_call(functools.partial(kernel, nz, nx, rows, chans), out_shape=...]
    unnamed x6 -> x1, local copies, waits for them, and re-layouts: 3.26 us -> 1.67 us
    sub x1 -> x0, other arithmetic: 0.76 us -> none  [depth_mask(): lower = middle - DEPTH_BLOCK * row_counts]
    select_n x1 -> x0, other arithmetic: 0.73 us -> none  [kernel_shards(): return jnp.where(depth_mask(row_counts), spectrum, jnp.zeros_like(spectrum))]
where the time goes in v2:
time: 31.3 us; the launch traced here: 31.2 us
  Pallas kernels  29.5 us (94%)
  local copies, waits for them, and re-layouts  1.67 us (5%)
    pallas_call x1, Pallas kernels, kernel_shards(): pl.pallas_call(functools.partial(kernel, nz, nx, rows, chans), out_shape=...  29.5 us
    unnamed x1, local copies, waits for them, and re-layouts  1.67 us

profile of v2, /device:TPU:0, one launch (start us, length us, event | category | flops | bytes accessed | tf_op | source)
XLA Modules:
  0.0 31.2 jit_solution(12817438921023012099)
XLA Ops:
  0.0 29.5 %shard_map.46 = f32[32,2048]{1,0:T(8,128)} custom-call(bf16[4,2,2,32,2048]{4,3,2,1,0:T(8,128)(2,1)} %bitcast.4, f32[128,128]{1,0:T(8,128)} %bitcast.5, s32[128,128]{1,0:T(8,128)} %bitcast.6, s32[4,128]{1,0:T(4,128)} %bitcast.7), custom_call_target="tpu_custom_call" | custom-call | flops 4294967296 | bytes 2097152 | tf_op jit(solution)/shard_map/pallas_call | solution.py:345
  29.5 1.7 %copy.6 = f32[32,2048]{1,0:T(8,128)} copy(f32[32,2048]{1,0:T(8,128)} %shard_map.46) | data formatting | bytes 524288

commit v3 on v2

--- a/solution.py
+++ b/solution.py
@@ -86,6 +86,9 @@
 LANES = 128
 PORTIONS = 4
 COLS = NPHI // PORTIONS
+SPLIT = 2
+PIECES = PORTIONS * SPLIT
+WIDE = COLS // SPLIT
 FINE = 64
 COARSE = NPHI // FINE
 
@@ -170,7 +173,7 @@
         [(lam_hbm, lam_ref), (flag_hbm, flag_ref), (count_hbm, count_ref)])]
     for copy in small:
         copy.start()
-    for xd in range(nx):
+    for xd in (1 - x, x):
         local_copy(xd).start()
 
     @pl.when(outer)
@@ -181,7 +184,7 @@
     def _():
         pl.semaphore_wait(barrier, 5)
 
-    for xd in range(nx):
+    for xd in (1 - x, x):
         pol_copy(xd).start()
 
     for copy in small:
@@ -229,19 +232,18 @@
             return carry
 
         lax.fori_loop(0, (COLS // FINE) * (chans // width), fill, 0)
-
-        @pl.when(j == 0)
-        def _():
-            for xd in range(nx):
-                local_copy(xd).wait()
-                pol_copy(xd).wait()
-
         sign = 1.0 - 2.0 * p.astype(jnp.float32)
         dims = (((1,), (1,)), ((), ()))
         half_rows = nz * rows
 
         def half(i, carry):
-            xd = lax.rem(1 - x + i + nx, nx)
+            xd = lax.rem(1 - x + i, nx)
+
+            @pl.when(j == 0)
+            def _():
+                local_copy(xd).wait()
+                pol_copy(xd).wait()
+
             both = data[:, xd].reshape(2 * half_rows, chans)
             first = lax.dot_general(both, table[0], dims, preferred_element_type=jnp.float32)
             second = lax.dot_general(both, table[1], dims, preferred_element_type=jnp.float32)
@@ -250,14 +252,16 @@
 
             @pl.when(i == 0)
             def _():
-                xout[j, 0] = real.astype(jnp.bfloat16)
-                xout[j, 1] = imag.astype(jnp.bfloat16)
-                x_copy(j).start()
+                for h in range(SPLIT):
+                    xout[j * SPLIT + h, 0] = real[:, h * WIDE:h * WIDE + WIDE].astype(jnp.bfloat16)
+                    xout[j * SPLIT + h, 1] = imag[:, h * WIDE:h * WIDE + WIDE].astype(jnp.bfloat16)
+                    x_copy(j * SPLIT + h).start()
 
             @pl.when(i == 1)
             def _():
-                sums[j, 0] = real
-                sums[j, 1] = imag
+                for h in range(SPLIT):
+                    sums[j * SPLIT + h, 0] = real[:, h * WIDE:h * WIDE + WIDE]
+                    sums[j * SPLIT + h, 1] = imag[:, h * WIDE:h * WIDE + WIDE]
 
             return carry
 
@@ -296,11 +300,11 @@
 
     def finish(j):
         value = total(j, z) + arrived(j, 0) + arrived(j, 3)
-        depth_id = j * COLS + lax.broadcasted_iota(jnp.int32, (rows, COLS), 1)
+        depth_id = j * WIDE + lax.broadcasted_iota(jnp.int32, (rows, WIDE), 1)
         inside = (depth_id >= NPHI // 2 - DEPTH_BLOCK * row_counts) & (
             depth_id < NPHI // 2 + DEPTH_BLOCK * row_counts)
         for part in range(2):
-            columns = pl.ds(pl.multiple_of(part * NPHI + j * COLS, COLS), COLS)
+            columns = pl.ds(pl.multiple_of(part * NPHI + j * WIDE, WIDE), WIDE)
             out_ref[:, columns] = jnp.where(inside, value[part], 0.0)
 
     owner = (z * nx + x) * 2 + p
@@ -311,21 +315,32 @@
     row_counts = jnp.sum(jnp.where(lane_id == own_lane, count_row, 0), 1, keepdims=True)
 
     def stage(i, carry):
-        @pl.when(i < PORTIONS)
+        compute(i)
+
+        @pl.when(i >= 2)
         def _():
-            compute(i)
-
-        def late(lag, action):
-            @pl.when((i >= lag) & (i < PORTIONS + lag))
-            def _():
-                action(i - lag)
-
-        late(1, after_x)
-        late(2, hop)
-        late(3, finish)
+            for h in range(SPLIT):
+                after_x((i - 2) * SPLIT + h)
+
+        @pl.when(i >= 3)
+        def _():
+            for h in range(SPLIT):
+                hop((i - 3) * SPLIT + h)
+
         return carry
 
-    lax.fori_loop(0, PORTIONS + 3, stage, 0)
+    lax.fori_loop(0, PORTIONS, stage, 0)
+
+    for q in range((PORTIONS - 2) * SPLIT, PIECES):
+        after_x(q)
+        hop(q - SPLIT)
+    for q in range(PIECES - 2 * SPLIT):
+        finish(q)
+    for q in range(PIECES - SPLIT, PIECES):
+        hop(q)
+        finish(q - SPLIT)
+    for q in range(PIECES - SPLIT, PIECES):
+        finish(q)
 
     def drain(j, carry):
         x_copy(j).wait_send()
@@ -333,7 +348,7 @@
             z_copy(j, taken, 0, far_in).wait_send()
         return carry
 
-    lax.fori_loop(0, PORTIONS, drain, 0)
+    lax.fori_loop(0, PIECES, drain, 0)
 
 
 def kernel_shards(nz, nx, stokes, lambda_sq, channel_flags, counts):
@@ -355,14 +370,14 @@
             pltpu.VMEM((2, FINE, chans), f32),
             pltpu.VMEM((2, COARSE, chans), f32),
             pltpu.VMEM((2, COLS, chans), bf16),
-            pltpu.VMEM((PORTIONS, 2, nz * rows, COLS), f32),
-            pltpu.VMEM((PORTIONS, 2, nz * rows, COLS), bf16),
-            pltpu.VMEM((PORTIONS, 2, nz * rows, COLS), bf16),
-            pltpu.VMEM((PORTIONS, 3, 2, rows, COLS), bf16),
-            pltpu.VMEM((PORTIONS, 4, 2, rows, COLS), bf16),
+            pltpu.VMEM((PIECES, 2, nz * rows, WIDE), f32),
+            pltpu.VMEM((PIECES, 2, nz * rows, WIDE), bf16),
+            pltpu.VMEM((PIECES, 2, nz * rows, WIDE), bf16),
+            pltpu.VMEM((PIECES, 3, 2, rows, WIDE), bf16),
+            pltpu.VMEM((PIECES, 4, 2, rows, WIDE), bf16),
             DMA((3,)), DMA((nx,)), DMA((nx,)), DMA((nx,)),
-            DMA((PORTIONS,)), DMA((PORTIONS,)),
-            DMA((PORTIONS, 3)), DMA((PORTIONS, 4)),
+            DMA((PIECES,)), DMA((PIECES,)),
+            DMA((PIECES, 3)), DMA((PIECES, 4)),
         ],
         compiler_params=pltpu.CompilerParams(
             collective_id=0, has_side_effects=True, vmem_limit_bytes=VMEM_BYTES),

time: 31.3 us -> 30.2 us (0.965)
  Pallas kernels: 29.5 us -> 28.4 us
    pallas_call x1, Pallas kernels: 29.5 us -> 28.4 us  [kernel_shards(): pl.pallas_call(functools.partial(kernel, nz, nx, rows, chans), out_shape=...]
where the time goes in v3:
time: 30.2 us; the launch traced here: 30.1 us
  Pallas kernels  28.4 us (94%)
  local copies, waits for them, and re-layouts  1.67 us (6%)
    pallas_call x1, Pallas kernels, kernel_shards(): pl.pallas_call(functools.partial(kernel, nz, nx, rows, chans), out_shape=...  28.4 us
    unnamed x1, local copies, waits for them, and re-layouts  1.67 us

profile of v3, /device:TPU:0, one launch (start us, length us, event | category | flops | bytes accessed | tf_op | source)
XLA Modules:
  0.0 30.1 jit_solution(3108426671079968958)
XLA Ops:
  0.0 28.4 %shard_map.46 = f32[32,2048]{1,0:T(8,128)} custom-call(bf16[4,2,2,32,2048]{4,3,2,1,0:T(8,128)(2,1)} %bitcast.4, f32[128,128]{1,0:T(8,128)} %bitcast.5, s32[128,128]{1,0:T(8,128)} %bitcast.6, s32[4,128]{1,0:T(4,128)} %bitcast.7), custom_call_target="tpu_custom_call" | custom-call | flops 4294967296 | bytes 2097152 | tf_op jit(solution)/shard_map/pallas_call | solution.py:360
  28.4 1.7 %copy.6 = f32[32,2048]{1,0:T(8,128)} copy(f32[32,2048]{1,0:T(8,128)} %shard_map.46) | data formatting | bytes 524288

commit v4 on v3

--- a/solution.py
+++ b/solution.py
@@ -89,6 +89,7 @@
 SPLIT = 2
 PIECES = PORTIONS * SPLIT
 WIDE = COLS // SPLIT
+TURNED = 5
 FINE = 64
 COARSE = NPHI // FINE
 
@@ -119,7 +120,9 @@
            stokes_ref, lam_hbm, flag_hbm, count_hbm, out_ref,
            lam_ref, flag_ref, count_ref,
            data, fine, coarse, table, sums, xout, xin, zout, zin,
-           small_sem, local_sem, pol_send, pol_recv, x_send, x_recv, z_send, z_recv):
+           turned, turned_end, turned_xout, turned_xin, turned_zout, turned_zin,
+           small_sem, local_sem, pol_send, pol_recv, x_send, x_recv, z_send, z_recv,
+           turned_x_send, turned_x_recv, turned_z_send, turned_z_recv):
     z = lax.axis_index("beam")
     x = lax.axis_index("slab")
     p = lax.axis_index("pol")
@@ -167,6 +170,17 @@
         return pltpu.make_async_remote_copy(
             src_ref=zout.at[j, taken], dst_ref=zin.at[j, slot],
             send_sem=z_send.at[j, taken], recv_sem=z_recv.at[j, slot],
+            device_id={"beam": to}, device_id_type=MESH)
+
+    def turned_x_copy():
+        return pltpu.make_async_remote_copy(
+            src_ref=turned_xout, dst_ref=turned_xin, send_sem=turned_x_send, recv_sem=turned_x_recv,
+            device_id={"slab": 1 - x}, device_id_type=MESH)
+
+    def turned_z_copy(taken, slot, to):
+        return pltpu.make_async_remote_copy(
+            src_ref=turned_zout.at[taken], dst_ref=turned_zin.at[slot],
+            send_sem=turned_z_send.at[taken], recv_sem=turned_z_recv.at[slot],
             device_id={"beam": to}, device_id_type=MESH)
 
     small = [pltpu.make_async_copy(source, held, small_sem.at[i]) for i, (source, held) in enumerate(
@@ -250,9 +264,15 @@
             real = first[:half_rows] + second[half_rows:]
             imag = sign * (first[half_rows:] - second[:half_rows])
 
-            @pl.when(i == 0)
+            @pl.when(j == TURNED // SPLIT)
             def _():
-                for h in range(SPLIT):
+                start = TURNED % SPLIT * WIDE
+                turned[xd, 0] = real[:, start:start + WIDE]
+                turned[xd, 1] = imag[:, start:start + WIDE]
+
+            for h in range(SPLIT):
+                @pl.when((i == 0) & (j * SPLIT + h != TURNED))
+                def _():
                     xout[j * SPLIT + h, 0] = real[:, h * WIDE:h * WIDE + WIDE].astype(jnp.bfloat16)
                     xout[j * SPLIT + h, 1] = imag[:, h * WIDE:h * WIDE + WIDE].astype(jnp.bfloat16)
                     x_copy(j * SPLIT + h).start()
@@ -298,8 +318,47 @@
             send(j, 1, 3, far_out, total(j, far_out) + arrived(j, 2))
             send(j, 2, 3, far_in, total(j, far_in) + arrived(j, 1))
 
+    def turned_total(d):
+        return turned[:, :, pl.ds(pl.multiple_of(d * rows, rows), rows), :]
+
+    def turned_send(taken, slot, to, value):
+        turned_zout[taken] = value.astype(jnp.bfloat16)
+        turned_z_copy(taken, slot, to).start()
+
+    def turned_arrived(slot):
+        turned_z_copy(0, slot, far_in).wait_recv()
+        return turned_zin[slot].astype(jnp.float32)
+
+    def turned_begin():
+        @pl.when(outer)
+        def _():
+            turned_send(0, 2, near_in, turned_total(far_out))
+            turned_send(1, 1, near_in, turned_total(far_in))
+            turned_send(2, 0, near_in, turned_total(near_in))
+
+        @pl.when(jnp.logical_not(outer))
+        def _():
+            turned_send(0, 0, near_out, turned_total(near_out))
+
+    def turned_hop():
+        @pl.when(jnp.logical_not(outer))
+        def _():
+            turned_send(1, 3, far_out, turned_total(far_out) + turned_arrived(2))
+            turned_send(2, 3, far_in, turned_total(far_in) + turned_arrived(1))
+
+    def turned_over_x():
+        turned_end[...] = turned_total(z) + turned_arrived(0) + turned_arrived(3)
+        turned_xout[...] = turned_end[1 - x].astype(jnp.bfloat16)
+        turned_x_copy().start()
+
+    def turned_finish():
+        turned_x_copy().wait_recv()
+        write(TURNED, turned_end[x] + turned_xin[...].astype(jnp.float32))
+
     def finish(j):
-        value = total(j, z) + arrived(j, 0) + arrived(j, 3)
+        write(j, total(j, z) + arrived(j, 0) + arrived(j, 3))
+
+    def write(j, value):
         depth_id = j * WIDE + lax.broadcasted_iota(jnp.int32, (rows, WIDE), 1)
         inside = (depth_id >= NPHI // 2 - DEPTH_BLOCK * row_counts) & (
             depth_id < NPHI // 2 + DEPTH_BLOCK * row_counts)
@@ -317,38 +376,60 @@
     def stage(i, carry):
         compute(i)
 
-        @pl.when(i >= 2)
-        def _():
-            for h in range(SPLIT):
-                after_x((i - 2) * SPLIT + h)
-
-        @pl.when(i >= 3)
-        def _():
-            for h in range(SPLIT):
-                hop((i - 3) * SPLIT + h)
+        @pl.when(i == 1)
+        def _():
+            after_x(0)
+
+        @pl.when(i == 2)
+        def _():
+            after_x(1)
+            turned_begin()
+            hop(0)
+
+        @pl.when(i == 3)
+        def _():
+            after_x(2)
+            after_x(3)
+            hop(1)
 
         return carry
 
     lax.fori_loop(0, PORTIONS, stage, 0)
 
-    for q in range((PORTIONS - 2) * SPLIT, PIECES):
-        after_x(q)
-        hop(q - SPLIT)
-    for q in range(PIECES - 2 * SPLIT):
-        finish(q)
-    for q in range(PIECES - SPLIT, PIECES):
-        hop(q)
-        finish(q - SPLIT)
-    for q in range(PIECES - SPLIT, PIECES):
-        finish(q)
+    after_x(4)
+    hop(2)
+    turned_hop()
+    hop(3)
+    finish(0)
+    after_x(6)
+    finish(1)
+    hop(4)
+    turned_over_x()
+    finish(2)
+    after_x(7)
+    finish(3)
+    hop(6)
+    finish(4)
+    hop(7)
+    turned_finish()
+    finish(6)
+    finish(7)
 
     def drain(j, carry):
-        x_copy(j).wait_send()
+        @pl.when(j != TURNED)
+        def _():
+            x_copy(j).wait_send()
+
         for taken in range(3):
-            z_copy(j, taken, 0, far_in).wait_send()
+            @pl.when(j != TURNED)
+            def _():
+                z_copy(j, taken, 0, far_in).wait_send()
         return carry
 
     lax.fori_loop(0, PIECES, drain, 0)
+    turned_x_copy().wait_send()
+    for taken in range(3):
+        turned_z_copy(taken, 0, far_in).wait_send()
 
 
 def kernel_shards(nz, nx, stokes, lambda_sq, channel_flags, counts):
@@ -375,9 +456,16 @@
             pltpu.VMEM((PIECES, 2, nz * rows, WIDE), bf16),
             pltpu.VMEM((PIECES, 3, 2, rows, WIDE), bf16),
             pltpu.VMEM((PIECES, 4, 2, rows, WIDE), bf16),
+            pltpu.VMEM((nx, 2, nz * rows, WIDE), f32),
+            pltpu.VMEM((nx, 2, rows, WIDE), f32),
+            pltpu.VMEM((2, rows, WIDE), bf16),
+            pltpu.VMEM((2, rows, WIDE), bf16),
+            pltpu.VMEM((3, nx, 2, rows, WIDE), bf16),
+            pltpu.VMEM((4, nx, 2, rows, WIDE), bf16),
             DMA((3,)), DMA((nx,)), DMA((nx,)), DMA((nx,)),
             DMA((PIECES,)), DMA((PIECES,)),
             DMA((PIECES, 3)), DMA((PIECES, 4)),
+            DMA, DMA, DMA((3,)), DMA((4,)),
         ],
         compiler_params=pltpu.CompilerParams(
             collective_id=0, has_side_effects=True, vmem_limit_bytes=VMEM_BYTES),

time: 30.2 us -> 32.4 us (1.073)
  Pallas kernels: 28.4 us -> 30.6 us
    pallas_call x1, Pallas kernels: 28.4 us -> 30.6 us  [kernel_shards(): pl.pallas_call(functools.partial(kernel, nz, nx, rows, chans), out_shape=...]
where the time goes in v4:
time: 32.4 us; the launch traced here: 32.3 us
  Pallas kernels  30.6 us (94%)
  local copies, waits for them, and re-layouts  1.67 us (5%)
    pallas_call x1, Pallas kernels, kernel_shards(): pl.pallas_call(functools.partial(kernel, nz, nx, rows, chans), out_shape=...  30.6 us
    unnamed x1, local copies, waits for them, and re-layouts  1.67 us

profile of v4, /device:TPU:0, one launch (start us, length us, event | category | flops | bytes accessed | tf_op | source)
XLA Modules:
  0.0 32.3 jit_solution(8196458004559519589)
XLA Ops:
  0.0 30.6 %shard_map.46 = f32[32,2048]{1,0:T(8,128)} custom-call(bf16[4,2,2,32,2048]{4,3,2,1,0:T(8,128)(2,1)} %bitcast.4, f32[128,128]{1,0:T(8,128)} %bitcast.5, s32[128,128]{1,0:T(8,128)} %bitcast.6, s32[4,128]{1,0:T(4,128)} %bitcast.7), custom_call_target="tpu_custom_call" | custom-call | flops 4294967296 | bytes 2097152 | tf_op jit(solution)/shard_map/pallas_call | solution.py:441
  30.6 1.7 %copy.6 = f32[32,2048]{1,0:T(8,128)} copy(f32[32,2048]{1,0:T(8,128)} %shard_map.46) | data formatting | bytes 524288

commit v5 on v3

--- a/solution.py
+++ b/solution.py
@@ -169,6 +169,12 @@
             send_sem=z_send.at[j, taken], recv_sem=z_recv.at[j, slot],
             device_id={"beam": to}, device_id_type=MESH)
 
+    def z_copy_all(j):
+        return pltpu.make_async_remote_copy(
+            src_ref=zout.at[j], dst_ref=zin.at[j, pl.ds(0, 3)],
+            send_sem=z_send.at[j, 0], recv_sem=z_recv.at[j, 0],
+            device_id={"beam": near_in}, device_id_type=MESH)
+
     small = [pltpu.make_async_copy(source, held, small_sem.at[i]) for i, (source, held) in enumerate(
         [(lam_hbm, lam_ref), (flag_hbm, flag_ref), (count_hbm, count_ref)])]
     for copy in small:
@@ -284,9 +290,10 @@
 
         @pl.when(outer)
         def _():
-            send(j, 0, 2, near_in, total(j, far_out))
-            send(j, 1, 1, near_in, total(j, far_in))
-            send(j, 2, 0, near_in, total(j, near_in))
+            zout[j, 0] = total(j, near_in).astype(jnp.bfloat16)
+            zout[j, 1] = total(j, far_in).astype(jnp.bfloat16)
+            zout[j, 2] = total(j, far_out).astype(jnp.bfloat16)
+            z_copy_all(j).start()
 
         @pl.when(jnp.logical_not(outer))
         def _():
@@ -295,11 +302,16 @@
     def hop(j):
         @pl.when(jnp.logical_not(outer))
         def _():
-            send(j, 1, 3, far_out, total(j, far_out) + arrived(j, 2))
-            send(j, 2, 3, far_in, total(j, far_in) + arrived(j, 1))
+            z_copy_all(j).wait_recv()
+            send(j, 1, 3, far_out, total(j, far_out) + zin[j, 2].astype(jnp.float32))
+            send(j, 2, 3, far_in, total(j, far_in) + zin[j, 1].astype(jnp.float32))
 
     def finish(j):
-        value = total(j, z) + arrived(j, 0) + arrived(j, 3)
+        @pl.when(outer)
+        def _():
+            z_copy(j, 0, 0, far_in).wait_recv()
+
+        value = total(j, z) + zin[j, 0].astype(jnp.float32) + arrived(j, 3)
         depth_id = j * WIDE + lax.broadcasted_iota(jnp.int32, (rows, WIDE), 1)
         inside = (depth_id >= NPHI // 2 - DEPTH_BLOCK * row_counts) & (
             depth_id < NPHI // 2 + DEPTH_BLOCK * row_counts)
@@ -344,8 +356,15 @@
 
     def drain(j, carry):
         x_copy(j).wait_send()
-        for taken in range(3):
-            z_copy(j, taken, 0, far_in).wait_send()
+
+        @pl.when(outer)
+        def _():
+            z_copy_all(j).wait_send()
+
+        @pl.when(jnp.logical_not(outer))
+        def _():
+            for taken in range(3):
+                z_copy(j, taken, 0, far_in).wait_send()
         return carry
 
     lax.fori_loop(0, PIECES, drain, 0)

time: 30.2 us -> 30.5 us (level)
  no operation moved by 1% of the time
where the time goes in v5:
time: 30.5 us; the launch traced here: 30.4 us
  Pallas kernels  28.7 us (94%)
  local copies, waits for them, and re-layouts  1.67 us (5%)
    pallas_call x1, Pallas kernels, kernel_shards(): pl.pallas_call(functools.partial(kernel, nz, nx, rows, chans), out_shape=...  28.7 us
    unnamed x1, local copies, waits for them, and re-layouts  1.67 us

profile of v5, /device:TPU:0, one launch (start us, length us, event | category | flops | bytes accessed | tf_op | source)
XLA Modules:
  0.0 30.4 jit_solution(16751827980083284851)
XLA Ops:
  0.0 28.7 %shard_map.46 = f32[32,2048]{1,0:T(8,128)} custom-call(bf16[4,2,2,32,2048]{4,3,2,1,0:T(8,128)(2,1)} %bitcast.4, f32[128,128]{1,0:T(8,128)} %bitcast.5, s32[128,128]{1,0:T(8,128)} %bitcast.6, s32[4,128]{1,0:T(4,128)} %bitcast.7), custom_call_target="tpu_custom_call" | custom-call | flops 4294967296 | bytes 2097152 | tf_op jit(solution)/shard_map/pallas_call | solution.py:379
  28.7 1.7 %copy.6 = f32[32,2048]{1,0:T(8,128)} copy(f32[32,2048]{1,0:T(8,128)} %shard_map.46) | data formatting | bytes 524288
